TPU v7x, 256 devices: a whole 4x4x8 slice. The times are simulated.
256 devices in a mesh: replica: 32 (over x, y, core), fsdp: 8 (over z).
Axes of the slice: x: 4, y: 4, z: 8, core: 2. Of those that a mesh axis runs over, the one named last changes fastest.
Arguments:
- key_delta: float32 [32, 4096, 1024], P('replica', 'fsdp')
- gain_delta: float32 [32, 4096], P('replica', 'fsdp')
- key_params: float32 [4096, 1024], P('fsdp'), may hold values from -6 to 6
- key_moment: float32 [4096, 1024], P('fsdp'), may hold values from -6 to 6
- gain_params: float32 [4096], P('fsdp'), may hold values from 0.1 to 1.9
- gain_moment: float32 [4096], P('fsdp'), may hold values from -6 to 6
Outputs:
- key_new: float32 [4096, 1024], P('fsdp')
- key_moment_new: float32 [4096, 1024], P('fsdp')
- gain_new: float32 [4096], P('fsdp')
- gain_moment_new: float32 [4096], P('fsdp')
All inputs are finite; a program needn't handle non-finite values.
Results may differ from a plain program's by a relative error of at most 0.00002.
Values sent between devices are 32-bit elements; how exact they have to be, the bound alone decides.
A program may use at most 64 MiB of HBM per device.

v0:
```python
import jax
import jax.numpy as jnp
from jax import lax
from jax.sharding import PartitionSpec as P

D = 4096
KV = 1024


def moment_step(delta_sum, moment, workers):
    average = delta_sum / workers
    moment_new = 0.9 * moment + average
    return (moment_new, average + 0.9 * moment_new)


def apply_step(params, step_value, square_sum, count):
    rms_value = jnp.sqrt(square_sum / count + 1e-06)
    return params - 0.7 * step_value / rms_value


def on_device(key_delta, gain_delta, key_params, key_moment, gain_params, gain_moment):
    workers = lax.axis_size("replica")
    key_local = key_delta[0]
    gain_local = gain_delta[0]
    key_sum, gain_sum = (
        lax.psum_scatter(key_local, "replica", scatter_dimension=0, tiled=True),
        lax.psum_scatter(gain_local, "replica", scatter_dimension=0, tiled=True),
    )
    owned = key_sum.shape[0]
    first = lax.axis_index("replica") * owned
    key_param_rows = lax.dynamic_slice_in_dim(key_params, first, owned, 0)
    key_moment_rows = lax.dynamic_slice_in_dim(key_moment, first, owned, 0)
    gain_param_rows = lax.dynamic_slice_in_dim(gain_params, first, owned, 0)
    gain_moment_rows = lax.dynamic_slice_in_dim(gain_moment, first, owned, 0)
    key_mom, key_step = moment_step(key_sum, key_moment_rows, workers)
    gain_mom, gain_step = moment_step(gain_sum, gain_moment_rows, workers)
    key_squares, gain_squares = lax.psum(
        (jnp.sum(key_step * key_step), jnp.sum(gain_step * gain_step)), ("replica", "fsdp")
    )
    key_out = apply_step(key_param_rows, key_step, key_squares, D * KV)
    gain_out = apply_step(gain_param_rows, gain_step, gain_squares, D)
    key_new, key_moment_new, gain_new, gain_moment_new = (
        lax.all_gather(key_out, "replica", axis=0, tiled=True),
        lax.all_gather(key_mom, "replica", axis=0, tiled=True),
        lax.all_gather(gain_out, "replica", axis=0, tiled=True),
        lax.all_gather(gain_mom, "replica", axis=0, tiled=True),
    )
    return (key_new, key_moment_new, gain_new, gain_moment_new)


def solution(mesh):
    return jax.shard_map(
        on_device,
        mesh=mesh,
        in_specs=(
            P("replica", "fsdp", None),
            P("replica", "fsdp"),
            P("fsdp", None),
            P("fsdp", None),
            P("fsdp"),
            P("fsdp"),
        ),
        out_specs=(P("fsdp", None), P("fsdp", None), P("fsdp"), P("fsdp")),
        check_vma=False,
    )
```

profile of v0, /device:TPU:1, one launch (start us, length us, event | category | flops | bytes accessed | tf_op | source)
XLA Modules:
  0.0 323.4 jit_solution(8514693870691880425)
XLA Ops:
  7.2 0.0 copy-start.2
  7.2 0.0 copy-start.1
  7.2 0.0 reduce-scatter.2.cloned.1.call-start
  7.2 0.7 reduce-scatter.2.cloned.1.call-update
  7.9 0.0 all-gather.5.cloned.1.call-start
  8.0 92.5 %reduce-scatter.2.cloned.1.call-done = f32[16,1024]{1,0:T(8,128)} async-done(((f32[512,1024]{1,0:T(8,128)}), f32[16,1024]{1,0:T(8,128)}) %reduce-scatter.2.cloned.1.call-update) | async-done | bytes 65552 | tf_op jit(solution)/shard_map/reduce_scatter | solution.py:26
  100.5 2.1 multiply_reduce_fusion
  102.6 0.0 all-gather.5.cloned.1.call-update
  102.6 0.0 all-gather.3.cloned.1.call-start
  102.7 0.0 copy-done.2
  102.7 0.6 fusion.2
  104.6 0.0 copy-done.1
  104.6 64.4 %all-reduce.2 = f32[512]{0:T(512)S(1)} all-reduce(f32[512]{0:T(512)S(1)} %bitcast.5), channel_id=3, replica_groups=mesh['replica'=32,'fsdp'=8] {'replica'}, use_global_device_ids=true, to_apply=%region_3.0.clone | all-reduce | flops 512 | bytes 4096
  169.0 0.8 fusion.1
  169.8 0.7 multiply_reduce_fusion.1
  170.5 74.6 %all-reduce.3 = (f32[]{:T(128)}, f32[]{:T(128)}) all-reduce(f32[]{:T(128)} %get-tuple-element.10, f32[]{:T(128)} %multiply_reduce_fusion.1), channel_id=1, replica_groups=mesh['replica'=32,'fsdp'=8] {'replica','fsdp'}, use_global_device_ids=true, to_apply=%region_2.0 | all-reduce | flops 2 | bytes 16 | tf_op jit(solution)/shard_map/psum | solution.py:37
  245.8 1.6 divide_subtract_fusion
  247.4 0.0 all-gather.3.cloned.1.call-update
  248.1 0.9 fusion
  248.9 63.3 %all-reduce.4 = (f32[512]{0:T(512)}, f32[512]{0:T(512)}) all-reduce(f32[512]{0:T(512)S(1)} %fusion, f32[512]{0:T(512)S(1)} %get-tuple-element.8), channel_id=1, replica_groups=mesh['replica'=32,'fsdp'=8] {'replica'}, use_global_device_ids=true, to_apply=%add | all-reduce | flops 1024 | bytes 8192
  312.2 0.0 all-gather.5.cloned.1.call-done
  312.3 3.3 %copy.14 = f32[512,1024]{1,0:T(8,128)} copy(f32[512,1024]{1,0:T(8,128)} %all-gather.3.cloned.1.call-done) | data formatting | bytes 4194304
  315.6 0.0 copy-done
  315.6 1.3 copy.15
  (4 shorter events, 0.0 us)
Async XLA Ops:
  7.2 95.5 %copy-start.2 = (u32[256]{0:T(256)S(1)}, u32[256]{0:T(256)}, u32[]{:S(2)}) copy-start(u32[256]{0:T(256)} %constant.37) | copy-start | bytes 3076
  7.2 97.4 %copy-start.1 = (f32[1,512]{1,0:T(1,128)S(1)}, f32[1,512]{1,0:T(1,128)}, u32[]{:S(2)}) copy-start(f32[1,512]{1,0:T(1,128)} %param.7) | copy-start | bytes 6148
  7.2 93.3 %reduce-scatter.2.cloned.1.call-start = ((), (), s32[]{:S(2)}) async-start(), calls=%async_computation.1 | async-start | bytes 2162688 | tf_op jit(solution)/shard_map/reduce_scatter | solution.py:26
  7.9 304.3 %all-gather.5.cloned.1.call-start = ((), (), s32[]{:S(2)}) async-start(), calls=%async_computation.3 | async-start | bytes 2162688 | tf_op jit(solution)/shard_map/all_gather | solution.py:44
  102.6 209.6 %all-gather.3.cloned.1.call-start = ((), (), s32[]{:S(2)}) async-start(), calls=%async_computation.2 | async-start | bytes 2162688 | tf_op jit(solution)/shard_map/all_gather | solution.py:43
  312.3 3.3 %copy-start = (f32[512,1024]{1,0:T(8,128)S(1)}, f32[512,1024]{1,0:T(8,128)}, u32[]{:S(2)}) copy-start(f32[512,1024]{1,0:T(8,128)} %all-gather.5.cloned.1.call-done) | copy-start | bytes 6291460
Sparse Core Ops, SparseCore 0:
  11.9 88.6 reduce-scatter.1
  103.6 50.2 all-gather.4
  247.5 46.1 all-gather.2
where the time goes:
time: 324 us; the launch traced here: 323 us
  blocking collectives  202 us (62%)
  waiting for transfers between devices  93.2 us (29%)
  between operations  16.5 us (5%)
  other arithmetic  6.05 us (2%)
  local copies, waits for them, and re-layouts  5.24 us (2%)
    unnamed x2, blocking collectives  128 us
    reduce_scatter x1, waiting for transfers between devices, on_device(): lax.psum_scatter(key_local, 'replica', scatter_dimension=0, tiled=True)  92.5 us
    psum x1, blocking collectives, on_device(): lax.psum((jnp.sum(key_step * key_step), jnp.sum(gain_step * gain_step)),...  74.6 us
  transfers between devices with their start and end apart: 3, of which 1 were waited for; matrix products, arithmetic and copies ran while one was open for 1% of the time, Pallas kernels for 0%

commit v1 on v0

v1 whole, which is shorter than its diff:
```python
import functools

import jax
import jax.numpy as jnp
from jax import lax
from jax.experimental import pallas as pl
from jax.experimental.pallas import tpu as pltpu
from jax.sharding import PartitionSpec as P

D = 4096
KV = 1024
NREP = 32
XS, YS, CORES, ZS = 4, 4, 2, 8
ROWS = D // ZS
HALF = ROWS // CORES
CHUNKS = 2
CROWS = HALF // CHUNKS
BROWS = CROWS // 2 // XS
PCOLS = KV // YS
MESH = pl.DeviceIdType.MESH


def update_kernel(
    kd, gd, kp_hbm, km_hbm, gp_hbm, gm_hbm,
    kn_out, kmn_out, gn_out, gmn_out,
    acc, r0, r1, r2, avg, kp, km,
    gd_v, gp_v, gm_v, g_core, g_x, g_y, s_z, s_y, s_x, s_c,
    load_sem, send_sem, sem0, sem1, sem2, sem3, sem4, sem5,
    gsend_sem, gc_sem, gx_sem, gy_sem, ssend_sem, sz_sem, sy_sem, sx_sem, sc_sem,
):
    r = lax.axis_index("replica")
    z = lax.axis_index("fsdp")
    x = r // (YS * CORES)
    y = (r // CORES) % YS
    c = r % CORES

    def at(px, py, pc):
        return ((px * YS + py) * CORES + pc, z)

    sibling = at(x, y, 1 - c)
    xpeer = [at((x + p) % XS, y, c) for p in range(1, XS)]
    ypeer = [at(x, (y + p) % YS, c) for p in range(1, YS)]
    zpeer = [(r, (z + p) % ZS) for p in range(1, ZS)]
    mine = pl.multiple_of(c * HALF, HALF)
    other = pl.multiple_of((1 - c) * HALF, HALF)

    def send(src, dst, ssem, rsem, device):
        cp = pltpu.make_async_remote_copy(
            src_ref=src, dst_ref=dst, send_sem=ssem, recv_sem=rsem,
            device_id=device, device_id_type=MESH,
        )
        cp.start()
        return cp

    loads = [
        pltpu.make_async_copy(kd.at[0, pl.ds(mine, HALF)], acc, load_sem.at[0]),
        pltpu.make_async_copy(gd, gd_v, load_sem.at[1]),
        pltpu.make_async_copy(gm_hbm, gm_v, load_sem.at[2]),
        pltpu.make_async_copy(gp_hbm, gp_v, load_sem.at[3]),
        pltpu.make_async_copy(km_hbm, km, load_sem.at[4]),
        pltpu.make_async_copy(kp_hbm, kp, load_sem.at[5]),
    ]
    for cp in loads:
        cp.start()

    barrier = pltpu.get_barrier_semaphore()
    partners = [sibling] + xpeer + ypeer + zpeer
    for device in partners:
        pl.semaphore_signal(barrier, inc=1, device_id=device, device_id_type=MESH)
    pl.semaphore_wait(barrier, len(partners))

    c0 = []
    for j in range(CHUNKS):
        c0.append(send(
            kd.at[0, pl.ds(other + j * CROWS, CROWS)],
            r0.at[pl.ds(j * CROWS, CROWS)], send_sem.at[0], sem0.at[j], sibling,
        ))
    loads[1].wait()
    gc = send(gd_v, g_core, gsend_sem.at[0], gc_sem, sibling)

    def block(j, o, q):
        return pl.multiple_of(j * CROWS + o * (CROWS // 2) + q * BROWS, 8)

    first = (x, y)
    second = (y, x)
    peers = ((xpeer, ypeer), (ypeer, xpeer))
    order = (1, 0, 2)

    loads[0].wait()
    c1 = {}
    for j in range(CHUNKS):
        c0[j].wait_recv()
        rows = pl.ds(j * CROWS, CROWS)
        acc[rows] = acc[rows] + r0[rows]
        for p in order:
            for o in range(2):
                q = (first[o] + p + 1) % 4
                c1[j, o, p] = send(
                    acc.at[pl.ds(block(j, o, q), BROWS)],
                    r1.at[p, j, o], send_sem.at[1], sem1.at[j, o, p], peers[o][0][p],
                )
        if j == 0:
            gc.wait_recv()
            g_x[x] = gd_v[...] + g_core[...]
            gx = [send(g_x.at[x], g_x.at[x], gsend_sem.at[1], gx_sem.at[p], xpeer[p]) for p in range(3)]
    for cp in gx:
        cp.wait_recv()
    g_y[y] = (g_x[0] + g_x[1]) + (g_x[2] + g_x[3])
    gy = [send(g_y.at[y], g_y.at[y], gsend_sem.at[2], gy_sem.at[p], ypeer[p]) for p in range(3)]

    def cols(q):
        return pl.ds(pl.multiple_of(q * PCOLS, PCOLS), PCOLS)

    c2 = {}
    for j in range(CHUNKS):
        for o in range(2):
            for p in order:
                c1[j, o, p].wait_recv()
            rows = pl.ds(block(j, o, first[o]), BROWS)
            acc[rows] = (acc[rows] + r1[0, j, o]) + (r1[1, j, o] + r1[2, j, o])
            for p in order:
                q = (second[o] + p + 1) % 4
                c2[j, o, p] = send(
                    acc.at[rows, cols(q)],
                    r2.at[p, j, o], send_sem.at[2], sem2.at[j, o, p], peers[o][1][p],
                )

    for cp in gy:
        cp.wait_recv()
    loads[2].wait()
    loads[3].wait()
    loads[4].wait()
    loads[5].wait()
    g_avg = ((g_y[0] + g_y[1]) + (g_y[2] + g_y[3])) * (1.0 / NREP)
    g_mom = 0.9 * gm_v[...] + g_avg
    g_step = g_avg + 0.9 * g_mom
    gmn_out[...] = g_mom
    g_sq = g_step * g_step
    g_part = (g_sq[:, 0:128] + g_sq[:, 128:256]) + (g_sq[:, 256:384] + g_sq[:, 384:512])

    c3 = {}
    k_part = jnp.zeros((1, 128), jnp.float32)
    for j in range(CHUNKS):
        for o in range(2):
            for p in order:
                c2[j, o, p].wait_recv()
            rows = pl.ds(block(j, o, first[o]), BROWS)
            piece = (acc[rows, cols(second[o])] + r2[0, j, o]) + (r2[1, j, o] + r2[2, j, o])
            piece = piece * (1.0 / NREP)
            arows = pl.ds(mine + block(j, o, first[o]), BROWS)
            avg[arows, cols(second[o])] = piece
            for p in order:
                part = avg.at[arows, cols(second[o])]
                c3[j, o, p] = send(part, part, send_sem.at[3], sem3.at[j, o, p], peers[o][1][p])
            step = piece + 0.9 * (0.9 * km[arows, cols(second[o])] + piece)
            sq = step * step
            k_part = k_part + jnp.sum(sq[:, :128] + sq[:, 128:], axis=0, keepdims=True)

    row = lax.broadcasted_iota(jnp.int32, (8, 128), 0)
    s_z[z] = jnp.where(row == 0, k_part, jnp.where(row == 1, g_part, 0.0))
    sz = [send(s_z.at[z], s_z.at[z], ssend_sem.at[0], sz_sem.at[p], zpeer[p]) for p in range(7)]

    c4 = {}
    for j in range(CHUNKS):
        for o in range(2):
            for p in order:
                c3[j, o, p].wait_recv()
            arows = pl.ds(mine + block(j, o, first[o]), BROWS)
            for p in order:
                part = avg.at[arows]
                c4[j, o, p] = send(part, part, send_sem.at[4], sem4.at[j, o, p], peers[o][0][p])

    for cp in sz:
        cp.wait_recv()
    s_y[y] = ((s_z[0] + s_z[1]) + (s_z[2] + s_z[3])) + ((s_z[4] + s_z[5]) + (s_z[6] + s_z[7]))
    sy = [send(s_y.at[y], s_y.at[y], ssend_sem.at[1], sy_sem.at[p], ypeer[p]) for p in range(3)]
    for cp in sy:
        cp.wait_recv()
    s_x[x] = (s_y[0] + s_y[1]) + (s_y[2] + s_y[3])
    sx = [send(s_x.at[x], s_x.at[x], ssend_sem.at[2], sx_sem.at[p], xpeer[p]) for p in range(3)]
    for cp in sx:
        cp.wait_recv()
    s_c[c] = (s_x[0] + s_x[1]) + (s_x[2] + s_x[3])
    sc = send(s_c.at[c], s_c.at[c], ssend_sem.at[3], sc_sem, sibling)

    g_all = (s_y[0] + s_y[0]) * 0.5
    g_total = jnp.sum(g_all[1:2, :])
    g_scale = 0.7 / jnp.sqrt(jnp.full((1, 128), g_total, jnp.float32) / D + 1e-06)
    gn_out[...] = gp_v[...] - g_step * jnp.concatenate([g_scale] * 4, axis=1)

    sc.wait_recv()
    k_total = jnp.sum(s_c[0, 0:1, :] + s_c[1, 0:1, :])
    k_scale = 0.7 / jnp.sqrt(jnp.full((8, 128), k_total, jnp.float32) / (D * KV) + 1e-06)
    k_scale = jnp.concatenate([k_scale] * (KV // 128), axis=1)

    def finish(base, rows):
        def step_rows(i, carry):
            at_rows = pl.ds(pl.multiple_of(base + i * 8, 8), 8)
            a = avg[at_rows]
            m = 0.9 * km[at_rows] + a
            kmn_out[at_rows] = m
            kn_out[at_rows] = kp[at_rows] - (a + 0.9 * m) * k_scale
            return carry
        lax.fori_loop(0, rows // 8, step_rows, 0, unroll=2)

    c5 = []
    for j in range(CHUNKS):
        for o in range(2):
            for p in order:
                c4[j, o, p].wait_recv()
        part = avg.at[pl.ds(mine + j * CROWS, CROWS)]
        c5.append(send(part, part, send_sem.at[0], sem5.at[j], sibling))
        finish(mine + j * CROWS, CROWS)
    for j in range(CHUNKS):
        c5[j].wait_recv()
        finish(other + j * CROWS, CROWS)

    for group in (c0, c1.values(), c2.values(), c3.values(), c4.values(), c5, [gc], gx, gy, sz, sy, sx, [sc]):
        for cp in group:
            cp.wait_send()


def on_device(key_delta, gain_delta, key_params, key_moment, gain_params, gain_moment):
    f32 = jnp.float32
    dma = pltpu.SemaphoreType.DMA
    hbm = pl.BlockSpec(memory_space=pltpu.HBM)
    vmem = pl.BlockSpec(memory_space=pltpu.VMEM)
    gl = ROWS
    kn, kmn, gn, gmn = pl.pallas_call(
        update_kernel,
        out_shape=(
            jax.ShapeDtypeStruct((ROWS, KV), f32),
            jax.ShapeDtypeStruct((ROWS, KV), f32),
            jax.ShapeDtypeStruct((1, gl), f32),
            jax.ShapeDtypeStruct((1, gl), f32),
        ),
        in_specs=[hbm] * 6,
        out_specs=[vmem] * 4,
        scratch_shapes=[
            pltpu.VMEM((HALF, KV), f32),
            pltpu.VMEM((HALF, KV), f32),
            pltpu.VMEM((3, CHUNKS, 2, BROWS, KV), f32),
            pltpu.VMEM((3, CHUNKS, 2, BROWS, PCOLS), f32),
            pltpu.VMEM((ROWS, KV), f32),
            pltpu.VMEM((ROWS, KV), f32),
            pltpu.VMEM((ROWS, KV), f32),
            pltpu.VMEM((1, gl), f32),
            pltpu.VMEM((1, gl), f32),
            pltpu.VMEM((1, gl), f32),
            pltpu.VMEM((1, gl), f32),
            pltpu.VMEM((4, 1, gl), f32),
            pltpu.VMEM((4, 1, gl), f32),
            pltpu.VMEM((8, 8, 128), f32),
            pltpu.VMEM((4, 8, 128), f32),
            pltpu.VMEM((4, 8, 128), f32),
            pltpu.VMEM((2, 8, 128), f32),
            dma((6,)),
            dma((5,)),
            dma((CHUNKS,)),
            dma((CHUNKS, 2, 3)),
            dma((CHUNKS, 2, 3)),
            dma((CHUNKS, 2, 3)),
            dma((CHUNKS, 2, 3)),
            dma((CHUNKS,)),
            dma((3,)),
            dma,
            dma((3,)),
            dma((3,)),
            dma((4,)),
            dma((7,)),
            dma((3,)),
            dma((3,)),
            dma,
        ],
        compiler_params=pltpu.CompilerParams(
            collective_id=0, has_side_effects=True, vmem_limit_bytes=40 << 20
        ),
        name="outer_update",
    )(
        key_delta, gain_delta, key_params, key_moment,
        gain_params.reshape(1, gl), gain_moment.reshape(1, gl),
    )
    return kn, kmn, gn.reshape(gl), gmn.reshape(gl)


def solution(mesh):
    return jax.shard_map(
        on_device,
        mesh=mesh,
        in_specs=(
            P("replica", "fsdp", None),
            P("replica", "fsdp"),
            P("fsdp", None),
            P("fsdp", None),
            P("fsdp"),
            P("fsdp"),
        ),
        out_specs=(P("fsdp", None), P("fsdp", None), P("fsdp"), P("fsdp")),
        check_vma=False,
    )
```

time: 324 us -> 52.9 us (0.16)
  blocking collectives: 202 us -> 0 us
  waiting for transfers between devices: 93.2 us -> 0 us
  Pallas kernels: 0 us -> 41.4 us
  between operations: 16.5 us -> 0.66 us
  other arithmetic: 6.05 us -> 0 us
  local copies, waits for them, and re-layouts: 5.24 us -> 10.6 us
    unnamed x2 -> x0, blocking collectives: 128 us -> none
    reduce_scatter x1 -> x0, waiting for transfers between devices: 92.5 us -> none  [on_device(): lax.psum_scatter(key_local, 'replica', scatter_dimension=0, tiled=True)]
    psum x1 -> x0, blocking collectives: 74.6 us -> none  [on_device(): lax.psum((jnp.sum(key_step * key_step), jnp.sum(gain_step * gain_step)),...]
    pallas_call x0 -> x1, Pallas kernels: none -> 41.4 us  [on_device(): pl.pallas_call(update_kernel, out_shape=(jax.ShapeDtypeStruct((ROWS, KV),...]
    unnamed x11 -> x16, local copies, waits for them, and re-layouts: 5.24 us -> 10.6 us
  transfers between devices with their start and end apart: 3 -> 0, of which waited for: 1 -> 0; matrix products, arithmetic and copies ran while one was open for 1% -> 0% of each run, Pallas kernels for 0% -> 0%
where the time goes in v1:
time: 52.9 us; the launch traced here: 52.6 us
  Pallas kernels  41.4 us (78%)
  local copies, waits for them, and re-layouts  10.6 us (20%)
  between operations  0.66 us (1%)
    pallas_call x1, Pallas kernels, on_device(): pl.pallas_call(update_kernel, out_shape=(jax.ShapeDtypeStruct((ROWS, KV),...  41.4 us
    unnamed x16, local copies, waits for them, and re-layouts  10.6 us

profile of v1, /device:TPU:1, one launch (start us, length us, event | category | flops | bytes accessed | tf_op | source)
XLA Modules:
  0.0 52.6 jit_solution(2930043456924668630)
XLA Ops:
  0.6 0.0 copy-start
  0.6 1.6 %copy-done = f32[1,512,1024]{2,1,0:T(8,128)S(1)} copy-done((f32[1,512,1024]{2,1,0:T(8,128)S(1)}, f32[1,512,1024]{2,1,0:T(8,128)}, u32[]{:S(2)}) %copy-start) | copy-done | bytes 2097176
  2.2 0.0 copy-start.1
  2.2 1.6 %copy-done.1 = f32[512,1024]{1,0:T(8,128)S(1)} copy-done((f32[512,1024]{1,0:T(8,128)S(1)}, f32[512,1024]{1,0:T(8,128)}, u32[]{:S(2)}) %copy-start.1) | copy-done | bytes 2097176
  3.8 0.0 copy-start.2
  3.8 1.6 %copy-done.2 = f32[512,1024]{1,0:T(8,128)S(1)} copy-done((f32[512,1024]{1,0:T(8,128)S(1)}, f32[512,1024]{1,0:T(8,128)}, u32[]{:S(2)}) %copy-start.2) | copy-done | bytes 2097176
  5.4 0.0 copy-start.3
  5.4 0.7 %copy-done.3 = f32[1,512]{1,0:T(1,128)S(1)} copy-done((f32[1,512]{1,0:T(1,128)S(1)}, f32[1,512]{1,0:T(1,128)}, u32[]{:S(2)}) %copy-start.3) | copy-done | bytes 2072
  6.1 0.0 copy-start.4
  6.1 0.7 %copy-done.4 = f32[512]{0:T(512)S(1)} copy-done((f32[512]{0:T(512)S(1)}, f32[512]{0:T(512)}, u32[]{:S(2)}) %copy-start.4) | copy-done | bytes 2072
  6.8 0.0 copy-start.5
  6.8 0.7 %copy-done.5 = f32[512]{0:T(512)S(1)} copy-done((f32[512]{0:T(512)S(1)}, f32[512]{0:T(512)}, u32[]{:S(2)}) %copy-start.5) | copy-done | bytes 2072
  7.5 41.4 %outer_update.1 = (f32[512,1024]{1,0:T(8,128)S(1)}, f32[512,1024]{1,0:T(8,128)S(1)}, f32[1,512]{1,0:T(1,128)S(1)}, f32[1,512]{1,0:T(1,128)S(1)}) custom-call(f32[1,512,1024]{2,1,0:T(8,128)S(1)} %copy-done, f32[1,512]{1,0:T(1,128)S(1)} %copy-done.3, f32[512,1024]{1,0:T(8,128)S(1)} %copy-done.1, f32[512,1024]{1,0:T(8,128)S(1)} %copy-done.2, ...), custom_call_target="tpu_custom_call" | custom-call | tf_op jit(solution)/shard_map/outer_update/pallas_call | solution.py:229
  48.8 1.3 %copy.14 = f32[512,1024]{1,0:T(8,128)} copy(f32[512,1024]{1,0:T(8,128)S(1)} %get-tuple-element.16) | data formatting | bytes 4194304
  50.1 1.3 %copy.15 = f32[512,1024]{1,0:T(8,128)} copy(f32[512,1024]{1,0:T(8,128)S(1)} %get-tuple-element.17) | data formatting | bytes 4194304
  51.5 0.6 %copy.16 = f32[512]{0:T(512)} copy(f32[512]{0:T(512)S(1)} %bitcast.7) | data formatting | bytes 4096
  52.0 0.6 %copy.17 = f32[512]{0:T(512)} copy(f32[512]{0:T(512)S(1)} %bitcast.6) | data formatting | bytes 4096
Async XLA Ops:
  0.6 1.6 %copy-start = (f32[1,512,1024]{2,1,0:T(8,128)S(1)}, f32[1,512,1024]{2,1,0:T(8,128)}, u32[]{:S(2)}) copy-start(f32[1,512,1024]{2,1,0:T(8,128)} %kd.1) | copy-start | bytes 6291460
  2.2 1.6 %copy-start.1 = (f32[512,1024]{1,0:T(8,128)S(1)}, f32[512,1024]{1,0:T(8,128)}, u32[]{:S(2)}) copy-start(f32[512,1024]{1,0:T(8,128)} %kp_hbm.1) | copy-start | bytes 6291460
  3.8 1.6 %copy-start.2 = (f32[512,1024]{1,0:T(8,128)S(1)}, f32[512,1024]{1,0:T(8,128)}, u32[]{:S(2)}) copy-start(f32[512,1024]{1,0:T(8,128)} %km_hbm.1) | copy-start | bytes 6291460
  5.4 0.7 %copy-start.3 = (f32[1,512]{1,0:T(1,128)S(1)}, f32[1,512]{1,0:T(1,128)}, u32[]{:S(2)}) copy-start(f32[1,512]{1,0:T(1,128)} %gd.1) | copy-start | bytes 6148
  6.1 0.7 %copy-start.4 = (f32[512]{0:T(512)S(1)}, f32[512]{0:T(512)}, u32[]{:S(2)}) copy-start(f32[512]{0:T(512)} %param.10) | copy-start | bytes 6148
  6.8 0.7 %copy-start.5 = (f32[512]{0:T(512)S(1)}, f32[512]{0:T(512)}, u32[]{:S(2)}) copy-start(f32[512]{0:T(512)} %param.11) | copy-start | bytes 6148

commit v2 on v1

v2 whole, which is shorter than its diff:
```python
import jax
import jax.numpy as jnp
from jax import lax
from jax.experimental import pallas as pl
from jax.experimental.pallas import tpu as pltpu
from jax.sharding import PartitionSpec as P

D = 4096
KV = 1024
NREP = 32
XS, YS, CORES, ZS = 4, 4, 2, 8
ROWS = D // ZS
HALF = ROWS // CORES
CHUNKS = 2
CROWS = HALF // CHUNKS
BROWS = CROWS // 2 // XS
PCOLS = KV // YS
TAIL = 8
MESH = pl.DeviceIdType.MESH


def comm_kernel(
    kd, gd, kp_hbm, km_hbm, gp_hbm, gm_hbm,
    mom, stp, kp, scale, gn_out, gmn_out,
    acc, r0, r1, r2, avg, km,
    gd_v, gp_v, gm_v, g_core, g_x, g_y, s_z, s_p,
    load_sem, send_sem, sem0, sem1, sem2, sem3, sem4, sem5,
    gsend_sem, gc_sem, gx_sem, gy_sem, ssend_sem, sz_sem, sp_sem,
):
    r = lax.axis_index("replica")
    z = lax.axis_index("fsdp")
    x = r // (YS * CORES)
    y = (r // CORES) % YS
    c = r % CORES

    def at(px, py, pc):
        return ((px * YS + py) * CORES + pc, z)

    sibling = at(x, y, 1 - c)
    xpeer = [at((x + p) % XS, y, c) for p in (1, 2, 3)]
    ypeer = [at(x, (y + p) % YS, c) for p in (1, 2, 3)]
    plane = [at((x + p) % XS, (y + q) % YS, c) for p in range(4) for q in range(4) if p or q]
    column = [
        (at(x, y, (c + q) % 2)[0], (z + p) % ZS) for p in range(ZS) for q in range(2) if p or q
    ]
    mine = pl.multiple_of(c * HALF, HALF)
    other = pl.multiple_of((1 - c) * HALF, HALF)

    def send(src, dst, ssem, rsem, device):
        pltpu.make_async_remote_copy(
            src_ref=src, dst_ref=dst, send_sem=ssem, recv_sem=rsem,
            device_id=device, device_id_type=MESH,
        ).start()

    def wait(sem, like):
        pltpu.make_async_copy(like, like, sem).wait()

    loads = [
        pltpu.make_async_copy(kd.at[0, pl.ds(mine, HALF)], acc, load_sem.at[0]),
        pltpu.make_async_copy(gd, gd_v, load_sem.at[1]),
        pltpu.make_async_copy(gm_hbm, gm_v, load_sem.at[2]),
        pltpu.make_async_copy(gp_hbm, gp_v, load_sem.at[3]),
        pltpu.make_async_copy(km_hbm, km, load_sem.at[4]),
        pltpu.make_async_copy(kp_hbm, kp, load_sem.at[5]),
    ]
    for cp in loads:
        cp.start()

    barrier = pltpu.get_barrier_semaphore()
    partners = plane + column
    for device in partners:
        pl.semaphore_signal(barrier, inc=1, device_id=device, device_id_type=MESH)
    pl.semaphore_wait(barrier, len(partners))

    for j in range(CHUNKS):
        send(
            kd.at[0, pl.ds(other + j * CROWS, CROWS)],
            r0.at[j], send_sem.at[0], sem0.at[j], sibling,
        )
    loads[1].wait()
    send(gd_v, g_core, gsend_sem.at[0], gc_sem, sibling)

    def block(j, o, q):
        return pl.multiple_of(j * CROWS + o * (CROWS // 2) + q * BROWS, 8)

    def cols(q):
        return pl.ds(pl.multiple_of(q * PCOLS, PCOLS), PCOLS)

    first = (x, y)
    second = (y, x)
    peers = ((xpeer, ypeer), (ypeer, xpeer))
    order = (1, 0, 2)

    loads[0].wait()
    for j in range(CHUNKS):
        wait(sem0.at[j], r0.at[j])
        rows = pl.ds(j * CROWS, CROWS)
        acc[rows] = acc[rows] + r0[j]
        for p in order:
            for o in range(2):
                q = (first[o] + p + 1) % 4
                send(
                    acc.at[pl.ds(block(j, o, q), BROWS)],
                    r1.at[j, o, p], send_sem.at[1], sem1.at[j, o], peers[o][0][p],
                )
        if j == 0:
            wait(gc_sem, g_core)
            g_x[x] = gd_v[...] + g_core[...]
            for p in range(3):
                send(g_x.at[x], g_x.at[x], gsend_sem.at[1], gx_sem, xpeer[p])
    wait(gx_sem, g_x.at[0:3])
    g_y[y] = (g_x[0] + g_x[1]) + (g_x[2] + g_x[3])
    for p in range(3):
        send(g_y.at[y], g_y.at[y], gsend_sem.at[2], gy_sem, ypeer[p])

    for j in range(CHUNKS):
        for o in range(2):
            wait(sem1.at[j, o], r1.at[j, o])
            rows = pl.ds(block(j, o, first[o]), BROWS)
            acc[rows] = (acc[rows] + r1[j, o, 0]) + (r1[j, o, 1] + r1[j, o, 2])
            for p in order:
                q = (second[o] + p + 1) % 4
                send(
                    acc.at[rows, cols(q)],
                    r2.at[j, o, p], send_sem.at[2], sem2.at[j, o], peers[o][1][p],
                )

    wait(gy_sem, g_y.at[0:3])
    for k in range(2, 6):
        loads[k].wait()
    g_avg = ((g_y[0] + g_y[1]) + (g_y[2] + g_y[3])) * (1.0 / NREP)
    g_mom = 0.9 * gm_v[...] + g_avg
    g_step = g_avg + 0.9 * g_mom
    gmn_out[...] = g_mom
    g_sq = g_step * g_step
    g_part = (g_sq[:, 0:128] + g_sq[:, 128:256]) + (g_sq[:, 256:384] + g_sq[:, 384:512])

    k_part = jnp.zeros((1, 128), jnp.float32)
    for j in range(CHUNKS):
        for o in range(2):
            wait(sem2.at[j, o], r2.at[j, o])
            own = cols(second[o])
            rows = pl.ds(block(j, o, first[o]), BROWS)
            piece = (acc[rows, own] + r2[j, o, 0]) + (r2[j, o, 1] + r2[j, o, 2])
            piece = piece * (1.0 / NREP)
            arows = pl.ds(mine + block(j, o, first[o]), BROWS)
            avg[arows, own] = piece
            for p in order:
                part = avg.at[arows, own]
                send(part, part, send_sem.at[3], sem3.at[j, o], peers[o][1][p])
            step = piece + 0.9 * (0.9 * km[arows, own] + piece)
            sq = step * step
            k_part = k_part + jnp.sum(sq[:, :128] + sq[:, 128:], axis=0, keepdims=True)

    row = lax.broadcasted_iota(jnp.int32, (8, 128), 0)
    own_z = z * CORES + c
    s_z[own_z] = jnp.where(row == 0, k_part, jnp.where(row == 1, g_part, 0.0))
    for device in column:
        send(s_z.at[own_z], s_z.at[own_z], ssend_sem.at[0], sz_sem, device)

    for j in range(CHUNKS):
        for o in range(2):
            wait(sem3.at[j, o], r2.at[j, o])
            part = avg.at[pl.ds(mine + block(j, o, first[o]), BROWS)]
            for p in order:
                send(part, part, send_sem.at[4], sem4.at[j, o], peers[o][0][p])

    wait(sz_sem, s_z.at[0:15])
    own_p = x * YS + y
    s_all = s_z[0]
    for k in range(1, ZS * CORES):
        s_all = s_all + s_z[k]
    s_p[own_p] = s_all
    for device in plane:
        send(s_p.at[own_p], s_p.at[own_p], ssend_sem.at[1], sp_sem, device)
    g_total = jnp.sum(s_all[1:2, :]) * 0.5
    g_scale = 0.7 / jnp.sqrt(jnp.full((1, 128), g_total, jnp.float32) / D + 1e-06)
    gn_out[...] = gp_v[...] - g_step * jnp.concatenate([g_scale] * 4, axis=1)

    def finish(base, rows):
        def step_rows(i, carry):
            at_rows = pl.ds(pl.multiple_of(base + i * 8, 8), 8)
            a = avg[at_rows]
            m = 0.9 * km[at_rows] + a
            mom[at_rows] = m
            stp[at_rows] = a + 0.9 * m
            return carry
        lax.fori_loop(0, rows // 8, step_rows, 0, unroll=2)

    for j in range(CHUNKS):
        for o in range(2):
            wait(sem4.at[j, o], r1.at[j, o])
        part = avg.at[pl.ds(mine + j * CROWS, CROWS)]
        send(part, part, send_sem.at[5], sem5.at[j], sibling)
        finish(mine + j * CROWS, CROWS)
    for j in range(CHUNKS):
        wait(sem5.at[j], r0.at[j])
        finish(other + j * CROWS, CROWS)

    wait(send_sem.at[0], r0)
    wait(send_sem.at[1], r1)
    wait(send_sem.at[2], r2)
    wait(send_sem.at[3], r2)
    wait(send_sem.at[4], r1)
    wait(send_sem.at[5], r0)
    wait(gsend_sem.at[0], g_core)
    wait(gsend_sem.at[1], g_x.at[0:3])
    wait(gsend_sem.at[2], g_y.at[0:3])
    wait(ssend_sem.at[0], s_z.at[0:15])
    wait(ssend_sem.at[1], s_p.at[0:15])
    wait(sp_sem, s_p.at[0:15])
    s_all = s_p[0]
    for k in range(1, XS * YS):
        s_all = s_all + s_p[k]
    k_total = jnp.sum(s_all[0:1, :])
    scale[...] = 0.7 / jnp.sqrt(jnp.full((8, 128), k_total, jnp.float32) / (D * KV) + 1e-06)


def tail_kernel(mom, stp, kp, scale, gn, gmn, kn_out, kmn_out, gn_out, gmn_out, kn, sem):
    copies = [
        pltpu.make_async_copy(mom, kmn_out, sem.at[0]),
        pltpu.make_async_copy(gn, gn_out, sem.at[1]),
        pltpu.make_async_copy(gmn, gmn_out, sem.at[2]),
    ]
    for cp in copies:
        cp.start()
    k_scale = jnp.concatenate([scale[...]] * (KV // 128), axis=1)
    size = ROWS // TAIL
    for t in range(TAIL):
        def step_rows(i, carry):
            rows = pl.ds(pl.multiple_of(t * size + i * 8, 8), 8)
            kn[rows] = kp[rows] - stp[rows] * k_scale
            return carry
        lax.fori_loop(0, size // 8, step_rows, 0, unroll=2)
        rows = pl.ds(t * size, size)
        cp = pltpu.make_async_copy(kn.at[rows], kn_out.at[rows], sem.at[3 + t])
        cp.start()
        copies.append(cp)
    for cp in copies:
        cp.wait()


def on_device(key_delta, gain_delta, key_params, key_moment, gain_params, gain_moment):
    f32 = jnp.float32
    dma = pltpu.SemaphoreType.DMA
    hbm = pl.BlockSpec(memory_space=pltpu.HBM)
    vmem = pl.BlockSpec(memory_space=pltpu.VMEM)
    gl = ROWS
    whole = jax.ShapeDtypeStruct((ROWS, KV), f32)
    line = jax.ShapeDtypeStruct((1, gl), f32)
    inputs = (
        key_delta, gain_delta, key_params, key_moment,
        gain_params.reshape(1, gl), gain_moment.reshape(1, gl),
    )
    inputs = tuple(pltpu.with_memory_space_constraint(a, pltpu.HBM) for a in inputs)
    parts = pl.pallas_call(
        comm_kernel,
        out_shape=(whole, whole, whole, jax.ShapeDtypeStruct((8, 128), f32), line, line),
        in_specs=[hbm] * 6,
        out_specs=[vmem] * 6,
        scratch_shapes=[
            pltpu.VMEM((HALF, KV), f32),
            pltpu.VMEM((CHUNKS, CROWS, KV), f32),
            pltpu.VMEM((CHUNKS, 2, 3, BROWS, KV), f32),
            pltpu.VMEM((CHUNKS, 2, 3, BROWS, PCOLS), f32),
            pltpu.VMEM((ROWS, KV), f32),
            pltpu.VMEM((ROWS, KV), f32),
            pltpu.VMEM((1, gl), f32),
            pltpu.VMEM((1, gl), f32),
            pltpu.VMEM((1, gl), f32),
            pltpu.VMEM((1, gl), f32),
            pltpu.VMEM((4, 1, gl), f32),
            pltpu.VMEM((4, 1, gl), f32),
            pltpu.VMEM((16, 8, 128), f32),
            pltpu.VMEM((16, 8, 128), f32),
            dma((6,)),
            dma((6,)),
            dma((CHUNKS,)),
            dma((CHUNKS, 2)),
            dma((CHUNKS, 2)),
            dma((CHUNKS, 2)),
            dma((CHUNKS, 2)),
            dma((CHUNKS,)),
            dma((3,)),
            dma,
            dma,
            dma,
            dma((2,)),
            dma,
            dma,
        ],
        compiler_params=pltpu.CompilerParams(
            collective_id=0, has_side_effects=True, vmem_limit_bytes=32 << 20
        ),
        name="worker_mean",
    )(*inputs)
    kn, kmn, gn, gmn = pl.pallas_call(
        tail_kernel,
        out_shape=(whole, whole, line, line),
        in_specs=[vmem] * 6,
        out_specs=[pl.BlockSpec(memory_space=pltpu.HBM)] * 4,
        scratch_shapes=[pltpu.VMEM((ROWS, KV), f32), dma((3 + TAIL,))],
        compiler_params=pltpu.CompilerParams(vmem_limit_bytes=32 << 20),
        name="apply_step",
    )(*parts)
    return kn, kmn, gn.reshape(gl), gmn.reshape(gl)


def solution(mesh):
    return jax.shard_map(
        on_device,
        mesh=mesh,
        in_specs=(
            P("replica", "fsdp", None),
            P("replica", "fsdp"),
            P("fsdp", None),
            P("fsdp", None),
            P("fsdp"),
            P("fsdp"),
        ),
        out_specs=(P("fsdp", None), P("fsdp", None), P("fsdp"), P("fsdp")),
        check_vma=False,
    )
```

time: 52.9 us -> 39.6 us (0.75)
  local copies, waits for them, and re-layouts: 10.6 us -> 0 us
  Pallas kernels: 41.4 us -> 38.9 us
    unnamed x16 -> x0, local copies, waits for them, and re-layouts: 10.6 us -> none
    pallas_call x1 -> x2, Pallas kernels: 41.4 us -> 38.9 us  [the longest x1 36.8 us: on_device(): pl.pallas_call(comm_kernel, out_shape=(whole, whole, whole, jax.ShapeDtyp...]
where the time goes in v2:
time: 39.6 us; the launch traced here: 39.5 us
  Pallas kernels  38.9 us (98%)
  between operations  0.64 us (2%)
    pallas_call x1, Pallas kernels, on_device(): pl.pallas_call(comm_kernel, out_shape=(whole, whole, whole, jax.ShapeDtyp...  36.8 us
    pallas_call x1, Pallas kernels, on_device(): pl.pallas_call(tail_kernel, out_shape=(whole, whole, line, line), in_spec...  2.1 us

profile of v2, /device:TPU:1, one launch (start us, length us, event | category | flops | bytes accessed | tf_op | source)
XLA Modules:
  0.0 39.5 jit_solution(3805958825699424942)
XLA Ops:
  0.6 36.8 %worker_mean.1 = (f32[512,1024]{1,0:T(8,128)S(1)}, f32[512,1024]{1,0:T(8,128)S(1)}, f32[512,1024]{1,0:T(8,128)S(1)}, f32[8,128]{1,0:T(8,128)S(1)}, f32[1,512]{1,0:T(1,128)S(1)}, /*index=5*/f32[1,512]{1,0:T(1,128)S(1)}) custom-call(f32[1,512,1024]{2,1,0:T(8,128)} %kd.1, f32[1,512]{1,0:T(1,128)} %gd.1, f32[512,1024]{1,0:T(8,128)} %kp_hbm.1, ...), custom_call_target="tpu_custom_call" | custom-call | tf_op jit(solution)/shard_map/worker_mean/pallas_call | solution.py:256
  37.4 2.1 %apply_step.1 = (f32[512,1024]{1,0:T(8,128)}, f32[512,1024]{1,0:T(8,128)}, f32[1,512]{1,0:T(1,128)}, f32[1,512]{1,0:T(1,128)}) custom-call(f32[512,1024]{1,0:T(8,128)S(1)} %get-tuple-element.14.mom, f32[512,1024]{1,0:T(8,128)S(1)} %get-tuple-element.15.stp, f32[512,1024]{1,0:T(8,128)S(1)} %get-tuple-element.16.kp, f32[8,128]{1,0:T(8,128)S(1)} %get-tuple-element.17.scale, ...), custom_call_target="tpu_custom_call" | custom-call | tf_op jit(solution)/shard_map/apply_step/pallas_call | solution.py:297

commit v3 on v0

v3 whole, which is shorter than its diff:
```python
import jax
import jax.numpy as jnp
from jax import lax
from jax.experimental import pallas as pl
from jax.experimental.pallas import tpu as pltpu
from jax.sharding import PartitionSpec as P

D = 4096
KV = 1024
NREP = 32
SIDE, CORES, ZS = 4, 2, 8
ROWS = D // ZS
BR = ROWS // (CORES * 2 * 2 * SIDE)
SHAPE = (CORES, 2, 2, SIDE, BR, KV)
OWN = SHAPE[1:]
CUTS = [(True, 0, 8, 0, 512), (True, 0, 8, 512, 512), (True, 8, 8, 0, 512), (False, 8, 8, 512, 512)]
CHUNKS = len(CUTS)
EARLY = ZS // 2
MESH = pl.DeviceIdType.MESH


def comm_kernel(
    kd, gd, kp_hbm, km_hbm, gm_hbm,
    mom, stp, kp, total, gmn_out, gstep_out,
    acc, r0, r1a, r1b, r1, c2, r2, c3, avg, km,
    gd_v, gm_v, g_core, g_x, g_y, s_z, s_p,
    load_sem, send_sem, sem0, sem1a, sem1b, sem1, sem2, sem3, sem4, sem5,
    gsend_sem, gc_sem, gx_sem, gy_sem, ssend_sem, sz_sem, sp_sem, ready_sem, go_sem,
):
    r = lax.axis_index("replica")
    z = lax.axis_index("fsdp")
    x = r // (SIDE * CORES)
    y = (r // CORES) % SIDE
    c = r % CORES

    def at(px, py, pc):
        return ((px * SIDE + py) * CORES + pc, z)

    sibling = at(x, y, 1 - c)
    xpeer = [at((x + p) % SIDE, y, c) for p in (1, 2, 3)]
    ypeer = [at(x, (y + p) % SIDE, c) for p in (1, 2, 3)]
    away = (2, 1, 3, 0)
    plane = [at((x + p) % SIDE, (y + q) % SIDE, c) for p in away for q in away if p or q]
    column = [
        (at(x, y, (c + q) % 2)[0], (z + p) % ZS)
        for p in (4, 3, 5, 2, 6, 1, 7, 0) for q in (1, 0) if p or q
    ]
    barrier = pltpu.get_barrier_semaphore()

    def greet(sem, device):
        pl.semaphore_signal(sem, inc=1, device_id=device, device_id_type=MESH)

    def greet_column(sem, k):
        for q in range(CORES):
            greet(sem, (at(x, y, q)[0], k))

    early = z < EARLY
    for device in [sibling] + xpeer + ypeer:
        greet(barrier, device)
    for k in range(1, ZS):
        pl.when(jnp.logical_and(k > z, early))(lambda: greet_column(barrier, k))

    loads = [
        pltpu.make_async_copy(kd.at[c], acc, load_sem.at[0]),
        pltpu.make_async_copy(gd, gd_v, load_sem.at[1]),
        pltpu.make_async_copy(gm_hbm, gm_v, load_sem.at[2]),
        pltpu.make_async_copy(km_hbm, km, load_sem.at[3]),
        pltpu.make_async_copy(kp_hbm, kp, load_sem.at[4]),
    ]
    for cp in loads[:3]:
        cp.start()

    def send(src, dst, ssem, rsem, device):
        pltpu.make_async_remote_copy(
            src_ref=src, dst_ref=dst, send_sem=ssem, recv_sem=rsem,
            device_id=device, device_id_type=MESH,
        ).start()

    def wait(sem, like):
        pltpu.make_async_copy(like, like, sem).wait()

    pl.semaphore_wait(barrier, 1 + 2 * (SIDE - 1) + CORES * jnp.minimum(z, EARLY))

    def cut(j):
        _, a, n, b, w = CUTS[j]
        return pl.ds(a, n), pl.ds(b, w)

    def piece(j, q):
        _, a, n, b, w = CUTS[j]
        return pl.ds(a, n), pl.ds(pl.multiple_of(b + q * (w // SIDE), 128), w // SIDE)

    def part(j):
        _, a, n, b, w = CUTS[j]
        return pl.ds(a, n), pl.ds(b // SIDE, w // SIDE)

    for j in range(CHUNKS):
        R, C = cut(j)
        for o in range(2):
            send(
                kd.at[1 - c, o, :, :, R, C], r0.at[o, :, :, R, C],
                send_sem.at[0], sem0.at[j, o], sibling,
            )
    loads[1].wait()
    send(gd_v, g_core, gsend_sem.at[0], gc_sem, sibling)
    for cp in loads[3:]:
        cp.start()
    for k in range(EARLY):
        pl.when(k < z)(lambda: greet_column(ready_sem, k))

    first = (x, y)
    second = (y, x)
    far = (ypeer, xpeer)

    def on_axis(o, q):
        return at(q, y, c) if o == 0 else at(x, q, c)

    def pairing(o, u):
        i = first[o]
        swap, mirror = i + 1 - 2 * (i % 2), 3 - i
        loc = (i + 1) % SIDE if u == 0 else i
        near, last = (swap, mirror) if u == 0 else (mirror, swap)
        base = 2 * (loc // 2)
        return dict(
            near=on_axis(o, near), last=on_axis(o, last), loc=loc,
            group=base, sent=2 - base, mate=2 * base + 1 - loc,
        )

    both = [(o, u) for o in range(2) for u in range(2)]
    pair = {ou: pairing(*ou) for ou in both}
    axis = (xpeer, ypeer)
    paired = [j for j in range(CHUNKS) if CUTS[j][0]]

    def place(j, o, u):
        return pair[o, u]["loc"] if CUTS[j][0] else first[o]

    loads[0].wait()
    for j in range(CHUNKS):
        R, C = cut(j)
        for o in range(2):
            wait(sem0.at[j, o], r0.at[o, :, :, R, C])
            acc[o, :, :, R, C] = acc[o, :, :, R, C] + r0[o, :, :, R, C]
            if CUTS[j][0]:
                for u in range(2):
                    p = pair[o, u]
                    send(
                        acc.at[o, u, pl.ds(p["sent"], 2), R, C], r1a.at[o, u, :, R, C],
                        send_sem.at[1], sem1a.at[j, o, u], p["near"],
                    )
            else:
                for p in (1, 0, 2):
                    send(
                        acc.at[o, :, (first[o] + p + 1) % SIDE, R, C], r1.at[o, p, :, R, C],
                        send_sem.at[6], sem1.at[j, o], axis[o][p],
                    )
        if j == 0:
            wait(gc_sem, g_core)
            g_x[x] = gd_v[...] + g_core[...]
            for device in xpeer:
                send(g_x.at[x], g_x.at[x], gsend_sem.at[1], gx_sem, device)
    wait(gx_sem, g_x.at[0:3])
    g_y[y] = (g_x[0] + g_x[1]) + (g_x[2] + g_x[3])
    for device in ypeer:
        send(g_y.at[y], g_y.at[y], gsend_sem.at[2], gy_sem, device)

    for j in paired:
        R, C = cut(j)
        for o, u in both:
            p = pair[o, u]
            group = pl.ds(p["group"], 2)
            wait(sem1a.at[j, o, u], r1a.at[o, u, :, R, C])
            acc[o, u, group, R, C] = acc[o, u, group, R, C] + r1a[o, u, :, R, C]
            send(
                acc.at[o, u, p["mate"], R, C], r1b.at[o, u, R, C],
                send_sem.at[2], sem1b.at[j, o, u], p["last"],
            )
    for j in range(CHUNKS):
        R, C = cut(j)
        for o in range(2):
            if CUTS[j][0]:
                for u in range(2):
                    wait(sem1b.at[j, o, u], r1b.at[o, u, R, C])
                    c2[o, u, R, C] = acc[o, u, pair[o, u]["loc"], R, C] + r1b[o, u, R, C]
            else:
                wait(sem1.at[j, o], r1.at[o, :, :, R, C])
                c2[o, :, R, C] = (acc[o, :, first[o], R, C] + r1[o, 0, :, R, C]) + (r1[o, 1, :, R, C] + r1[o, 2, :, R, C])
            for p in (1, 0, 2):
                Rq, Cq = piece(j, (second[o] + p + 1) % SIDE)
                Rp, Cp = part(j)
                send(
                    c2.at[o, :, Rq, Cq], r2.at[o, p, :, Rp, Cp],
                    send_sem.at[3], sem2.at[j, o], far[o][p],
                )

    wait(gy_sem, g_y.at[0:3])
    for cp in loads[2:]:
        cp.wait()
    g_avg = ((g_y[0] + g_y[1]) + (g_y[2] + g_y[3])) * (1.0 / NREP)
    g_mom = 0.9 * gm_v[...] + g_avg
    g_step = g_avg + 0.9 * g_mom
    gmn_out[...] = g_mom
    gstep_out[...] = g_step
    g_sq = g_step * g_step
    g_part = (g_sq[:, 0:128] + g_sq[:, 128:256]) + (g_sq[:, 256:384] + g_sq[:, 384:512])

    @pl.when(early)
    def _():
        pl.semaphore_wait(ready_sem, CORES * (ZS - 1 - z))

    @pl.when(z == 0)
    def _():
        for k in range(EARLY, ZS):
            greet(go_sem, (r, k))

    k_part = jnp.zeros((8, 128), jnp.float32)
    for j in range(CHUNKS):
        Rp, Cp = part(j)
        for o in range(2):
            wait(sem2.at[j, o], r2.at[o, :, :, Rp, Cp])
            Rq, Cq = piece(j, second[o])
            mean = (c2[o, :, Rq, Cq] + r2[o, 0, :, Rp, Cp]) + (r2[o, 1, :, Rp, Cp] + r2[o, 2, :, Rp, Cp])
            mean = mean * (1.0 / NREP)
            c3[o, :, Rq, Cq] = mean
            for p in (1, 0, 2):
                send(
                    c3.at[o, :, Rq, Cq], c3.at[o, :, Rq, Cq],
                    send_sem.at[4], sem3.at[j, o], far[o][p],
                )
            for u in range(2):
                step = mean[u] + 0.9 * (0.9 * km[c, o, u, place(j, o, u), Rq, Cq] + mean[u])
                square = step * step
                for a in range(0, step.shape[0], 8):
                    for b in range(0, step.shape[1], 128):
                        k_part = k_part + square[a:a + 8, b:b + 128]

    @pl.when(jnp.logical_not(early))
    def _():
        pl.semaphore_wait(go_sem, 1)

    own_z = z * CORES + c
    s_z[own_z, :, 0:128] = jnp.sum(k_part, axis=0, keepdims=True)
    s_z[own_z, :, 128:256] = g_part
    for device in column:
        send(s_z.at[own_z], s_z.at[own_z], ssend_sem.at[0], sz_sem, device)

    for j in range(CHUNKS):
        R, C = cut(j)
        for o in range(2):
            wait(sem3.at[j, o], r2.at[o, :, :, part(j)[0], part(j)[1]])
            for u in range(2):
                avg[c, o, u, place(j, o, u), R, C] = c3[o, u, R, C]
            for p in (1, 0, 2):
                for u in range(2):
                    send(
                        c3.at[o, u, R, C], avg.at[c, o, u, place(j, o, u), R, C],
                        send_sem.at[5], sem4.at[j, o], axis[o][p],
                    )

    def plane_round():
        wait(sz_sem, s_z.at[0:15])
        s_all = s_z[0]
        for k in range(1, ZS * CORES):
            s_all = s_all + s_z[k]
        own_p = x * SIDE + y
        s_p[own_p] = s_all[:, 0:128]
        total[:, 128:256] = s_all[:, 128:256]
        for device in plane:
            send(s_p.at[own_p], s_p.at[own_p], ssend_sem.at[1], sp_sem, device)

    def finish(side, o, j):
        R, C = cut(j)

        def block(i, carry):
            at_block = (side, o, i // SIDE, i % SIDE, R, C)
            a = avg[at_block]
            m = 0.9 * km[at_block] + a
            mom[at_block] = m
            stp[at_block] = a + 0.9 * m
            return carry
        lax.fori_loop(0, 2 * SIDE, block, 0, unroll=2)

    plane_round()
    for j in range(CHUNKS):
        R, C = cut(j)
        for o in range(2):
            wait(sem4.at[j, o], r1.at[o, :, :, R, C])
            blocks = avg.at[c, o, :, :, R, C]
            send(blocks, blocks, send_sem.at[7], sem5.at[j, o], sibling)
    for j in range(CHUNKS):
        for o in range(2):
            finish(c, o, j)
    for j in range(CHUNKS):
        R, C = cut(j)
        for o in range(2):
            wait(sem5.at[j, o], r0.at[o, :, :, R, C])
            finish(1 - c, o, j)

    def sent(sem, refs):
        for ref in refs:
            wait(sem, ref)

    straight = [j for j in range(CHUNKS) if not CUTS[j][0]]
    sent(send_sem.at[1], [r1a.at[:, :, :, cut(j)[0], cut(j)[1]] for j in paired])
    sent(send_sem.at[2], [r1b.at[:, :, cut(j)[0], cut(j)[1]] for j in paired])
    sent(send_sem.at[6], [r1.at[:, :, :, cut(j)[0], cut(j)[1]] for j in straight])
    wait(send_sem.at[5], r1)
    wait(send_sem.at[0], r0)
    wait(send_sem.at[3], r2)
    wait(send_sem.at[4], r2)
    wait(send_sem.at[7], r0)
    wait(gsend_sem.at[0], g_core)
    wait(gsend_sem.at[1], g_x.at[0:3])
    wait(gsend_sem.at[2], g_y.at[0:3])
    wait(ssend_sem.at[0], s_z.at[0:15])
    wait(ssend_sem.at[1], s_p.at[0:15])
    wait(sp_sem, s_p.at[0:15])
    s_all = s_p[0]
    for k in range(1, SIDE * SIDE):
        s_all = s_all + s_p[k]
    total[:, 0:128] = s_all


def tail_kernel(
    mom, stp, kp, total, gmn, g_step, gp_hbm, kn_out, kmn_out, gn_out, gmn_out, kn, gn, gp, sem
):
    load = pltpu.make_async_copy(gp_hbm, gp, sem.at[0])
    load.start()
    copies = [
        pltpu.make_async_copy(mom, kmn_out, sem.at[1]),
        pltpu.make_async_copy(gmn, gmn_out, sem.at[2]),
    ]
    for cp in copies:
        cp.start()
    k_sum = jnp.full((8, 128), jnp.sum(total[:, 0:128]), jnp.float32)
    k_scale = 0.7 / jnp.sqrt(k_sum / (D * KV) + 1e-06)
    k_scale = jnp.concatenate([k_scale] * (KV // 128), axis=1)
    k_scale = jnp.concatenate([k_scale] * (BR // 8), axis=0)
    for t in range(CORES * 2 * 2):
        blocks = (t // 4, t // 2 % 2, t % 2)

        def block(i, carry):
            kn[blocks + (i,)] = kp[blocks + (i,)] - stp[blocks + (i,)] * k_scale
            return carry
        lax.fori_loop(0, SIDE, block, 0)
        cp = pltpu.make_async_copy(kn.at[blocks], kn_out.at[blocks], sem.at[4 + t])
        cp.start()
        copies.append(cp)
    load.wait()
    g_sum = jnp.full((1, ROWS), jnp.sum(total[:, 128:256]) * (1.0 / CORES), jnp.float32)
    gn[...] = gp[...] - g_step[...] * (0.7 / jnp.sqrt(g_sum / D + 1e-06))
    cp = pltpu.make_async_copy(gn, gn_out, sem.at[3])
    cp.start()
    copies.append(cp)
    for cp in copies:
        cp.wait()


def on_device(key_delta, gain_delta, key_params, key_moment, gain_params, gain_moment):
    f32 = jnp.float32
    dma = pltpu.SemaphoreType.DMA
    signal = pltpu.SemaphoreType.REGULAR
    vector = pltpu.VMEM
    hbm = pl.BlockSpec(memory_space=pltpu.HBM)
    vmem = pl.BlockSpec(memory_space=pltpu.VMEM)
    whole = jax.ShapeDtypeStruct(SHAPE, f32)
    line = jax.ShapeDtypeStruct((1, ROWS), f32)
    hold = lambda a: pltpu.with_memory_space_constraint(a, pltpu.HBM)
    rows = lambda a: a.reshape(SHAPE)
    inputs = (rows(key_delta), gain_delta, rows(key_params), rows(key_moment), gain_moment.reshape(1, ROWS))
    parts = pl.pallas_call(
        comm_kernel,
        out_shape=(whole, whole, whole, jax.ShapeDtypeStruct((1, 256), f32), line, line),
        in_specs=[hbm] * 5,
        out_specs=[vmem] * 6,
        scratch_shapes=[
            vector(OWN, f32),
            vector(OWN, f32),
            vector((2, 2, 2, BR, KV), f32),
            vector((2, 2, BR, KV), f32),
            vector((2, 3, 2, BR, KV), f32),
            vector((2, 2, BR, KV), f32),
            vector((2, 3, 2, BR, KV // SIDE), f32),
            vector((2, 2, BR, KV), f32),
            vector(SHAPE, f32),
            vector(SHAPE, f32),
            vector((1, ROWS), f32),
            vector((1, ROWS), f32),
            vector((1, ROWS), f32),
            vector((4, 1, ROWS), f32),
            vector((4, 1, ROWS), f32),
            vector((16, 1, 256), f32),
            vector((16, 1, 128), f32),
            dma((5,)),
            dma((8,)),
            dma((CHUNKS, 2)),
            dma((CHUNKS, 2, 2)),
            dma((CHUNKS, 2, 2)),
            dma((CHUNKS, 2)),
            dma((CHUNKS, 2)),
            dma((CHUNKS, 2)),
            dma((CHUNKS, 2)),
            dma((CHUNKS, 2)),
            dma((3,)),
            dma,
            dma,
            dma,
            dma((2,)),
            dma,
            dma,
            signal,
            signal,
        ],
        compiler_params=pltpu.CompilerParams(
            collective_id=0, has_side_effects=True, vmem_limit_bytes=32 << 20
        ),
        name="worker_mean",
    )(*map(hold, inputs))
    kn, kmn, gn, gmn = pl.pallas_call(
        tail_kernel,
        out_shape=(whole, whole, line, line),
        in_specs=[vmem] * 6 + [hbm],
        out_specs=[hbm] * 4,
        scratch_shapes=[
            vector(SHAPE, f32),
            vector((1, ROWS), f32),
            vector((1, ROWS), f32),
            dma((4 + CORES * 2 * 2,)),
        ],
        compiler_params=pltpu.CompilerParams(vmem_limit_bytes=32 << 20),
        name="apply_step",
    )(*parts, hold(gain_params.reshape(1, ROWS)))
    return kn.reshape(ROWS, KV), kmn.reshape(ROWS, KV), gn.reshape(ROWS), gmn.reshape(ROWS)


def solution(mesh):
    return jax.shard_map(
        on_device,
        mesh=mesh,
        in_specs=(
            P("replica", "fsdp", None),
            P("replica", "fsdp"),
            P("fsdp", None),
            P("fsdp", None),
            P("fsdp"),
            P("fsdp"),
        ),
        out_specs=(P("fsdp", None), P("fsdp", None), P("fsdp"), P("fsdp")),
        check_vma=False,
    )
```

time: 324 us -> 34.1 us (0.11)
  blocking collectives: 202 us -> 0 us
  waiting for transfers between devices: 93.2 us -> 0 us
  Pallas kernels: 0 us -> 33.4 us
  between operations: 16.5 us -> 0.64 us
  other arithmetic: 6.05 us -> 0 us
  local copies, waits for them, and re-layouts: 5.24 us -> 0 us
    unnamed x2 -> x0, blocking collectives: 128 us -> none
    reduce_scatter x1 -> x0, waiting for transfers between devices: 92.5 us -> none  [on_device(): lax.psum_scatter(key_local, 'replica', scatter_dimension=0, tiled=True)]
    psum x1 -> x0, blocking collectives: 74.6 us -> none  [on_device(): lax.psum((jnp.sum(key_step * key_step), jnp.sum(gain_step * gain_step)),...]
    pallas_call x0 -> x2, Pallas kernels: none -> 33.4 us  [the longest x1 31.2 us: on_device(): pl.pallas_call(comm_kernel, out_shape=(whole, whole, whole, jax.ShapeDtyp...]
    unnamed x11 -> x0, local copies, waits for them, and re-layouts: 5.24 us -> none
  transfers between devices with their start and end apart: 3 -> 0, of which waited for: 1 -> 0; matrix products, arithmetic and copies ran while one was open for 1% -> 0% of each run, Pallas kernels for 0% -> 0%
where the time goes in v3:
time: 34.1 us; the launch traced here: 34 us
  Pallas kernels  33.4 us (98%)
  between operations  0.64 us (2%)
    pallas_call x1, Pallas kernels, on_device(): pl.pallas_call(comm_kernel, out_shape=(whole, whole, whole, jax.ShapeDtyp...  31.2 us
    pallas_call x1, Pallas kernels, on_device(): pl.pallas_call(tail_kernel, out_shape=(whole, whole, line, line), in_spec...  2.11 us

profile of v3, /device:TPU:1, one launch (start us, length us, event | category | flops | bytes accessed | tf_op | source)
XLA Modules:
  0.0 34.0 jit_solution(432999665317174954)
XLA Ops:
  0.6 31.2 %worker_mean.1 = (f32[2,2,2,4,16,1024]{5,4,3,2,1,0:T(8,128)S(1)}, f32[2,2,2,4,16,1024]{5,4,3,2,1,0:T(8,128)S(1)}, f32[2,2,2,4,16,1024]{5,4,3,2,1,0:T(8,128)S(1)}...) custom-call(f32[2,2,2,4,16,1024]{5,4,3,2,1,0:T(8,128)} %bitcast.9, f32[1,512]{1,0:T(1,128)} %gd.1, ...), custom_call_target="tpu_custom_call" | custom-call | tf_op jit(solution)/shard_map/worker_mean/pallas_call | solution.py:369
  31.9 2.1 %apply_step.1 = (f32[2,2,2,4,16,1024]{5,4,3,2,1,0:T(8,128)}, f32[2,2,2,4,16,1024]{5,4,3,2,1,0:T(8,128)}, f32[1,512]{1,0:T(1,128)}, f32[1,512]{1,0:T(1,128)}) custom-call(f32[2,2,2,4,16,1024]{5,4,3,2,1,0:T(8,128)S(1)} %get-tuple-element.14.mom, f32[2,2,2,4,16,1024]{5,4,3,2,1,0:T(8,128)S(1)} %get-tuple-element.15.stp, ...), custom_call_target="tpu_custom_call" | custom-call | tf_op jit(solution)/shard_map/apply_step/pallas_call | solution.py:417

commit v4 on v3

--- a/solution.py
+++ b/solution.py
@@ -16,6 +16,7 @@
 CUTS = [(True, 0, 8, 0, 512), (True, 0, 8, 512, 512), (True, 8, 8, 0, 512), (False, 8, 8, 512, 512)]
 CHUNKS = len(CUTS)
 EARLY = ZS // 2
+DIRECT = (1,)
 MESH = pl.DeviceIdType.MESH
 
 
@@ -23,9 +24,9 @@
     kd, gd, kp_hbm, km_hbm, gm_hbm,
     mom, stp, kp, total, gmn_out, gstep_out,
     acc, r0, r1a, r1b, r1, c2, r2, c3, avg, km,
-    gd_v, gm_v, g_core, g_x, g_y, s_z, s_p,
+    gd_v, gm_v, g_core, g_x, g_y, s_z, s_p, s_d,
     load_sem, send_sem, sem0, sem1a, sem1b, sem1, sem2, sem3, sem4, sem5,
-    gsend_sem, gc_sem, gx_sem, gy_sem, ssend_sem, sz_sem, sp_sem, ready_sem, go_sem,
+    gsend_sem, gc_sem, gx_sem, gy_sem, ssend_sem, sz_sem, sp_sem, sd_sem, ready_sem, go_sem,
 ):
     r = lax.axis_index("replica")
     z = lax.axis_index("fsdp")
@@ -206,11 +207,6 @@
     def _():
         pl.semaphore_wait(ready_sem, CORES * (ZS - 1 - z))
 
-    @pl.when(z == 0)
-    def _():
-        for k in range(EARLY, ZS):
-            greet(go_sem, (r, k))
-
     k_part = jnp.zeros((8, 128), jnp.float32)
     for j in range(CHUNKS):
         Rp, Cp = part(j)
@@ -231,14 +227,35 @@
                 for a in range(0, step.shape[0], 8):
                     for b in range(0, step.shape[1], 128):
                         k_part = k_part + square[a:a + 8, b:b + 128]
-
-    @pl.when(jnp.logical_not(early))
+        if j == 0:
+            @pl.when(z == 0)
+            def _():
+                for k in range(1, ZS):
+                    greet(go_sem, (r, k))
+
+    @pl.when(z > 0)
     def _():
         pl.semaphore_wait(go_sem, 1)
 
     own_z = z * CORES + c
-    s_z[own_z, :, 0:128] = jnp.sum(k_part, axis=0, keepdims=True)
+    own_p = x * SIDE + y
+    own_d = own_z * SIDE * SIDE + own_p
+    k_line = jnp.sum(k_part, axis=0, keepdims=True)
+    s_z[own_z, :, 0:128] = k_line
     s_z[own_z, :, 128:256] = g_part
+    at_zero = [jnp.logical_and(z == 0, r == d) for d in DIRECT]
+    direct = at_zero[0]
+    for here in at_zero[1:]:
+        direct = jnp.logical_or(direct, here)
+    for d, here in zip(DIRECT, at_zero):
+        @pl.when(jnp.logical_not(here))
+        def _():
+            send(s_z.at[own_z, :, pl.ds(0, 128)], s_d.at[own_d], ssend_sem.at[2], sd_sem, (d, 0))
+
+    @pl.when(direct)
+    def _():
+        s_d[own_d] = k_line
+
     for device in column:
         send(s_z.at[own_z], s_z.at[own_z], ssend_sem.at[0], sz_sem, device)
 
@@ -260,11 +277,16 @@
         s_all = s_z[0]
         for k in range(1, ZS * CORES):
             s_all = s_all + s_z[k]
-        own_p = x * SIDE + y
         s_p[own_p] = s_all[:, 0:128]
         total[:, 128:256] = s_all[:, 128:256]
         for device in plane:
-            send(s_p.at[own_p], s_p.at[own_p], ssend_sem.at[1], sp_sem, device)
+            skip = device[0] == DIRECT[0]
+            for d in DIRECT[1:]:
+                skip = jnp.logical_or(skip, device[0] == d)
+
+            @pl.when(jnp.logical_not(jnp.logical_and(z == 0, skip)))
+            def _():
+                send(s_p.at[own_p], s_p.at[own_p], ssend_sem.at[1], sp_sem, device)
 
     def finish(side, o, j):
         R, C = cut(j)
@@ -311,12 +333,36 @@
     wait(gsend_sem.at[1], g_x.at[0:3])
     wait(gsend_sem.at[2], g_y.at[0:3])
     wait(ssend_sem.at[0], s_z.at[0:15])
-    wait(ssend_sem.at[1], s_p.at[0:15])
-    wait(sp_sem, s_p.at[0:15])
-    s_all = s_p[0]
-    for k in range(1, SIDE * SIDE):
-        s_all = s_all + s_p[k]
-    total[:, 0:128] = s_all
+    wait(ssend_sem.at[1], s_p.at[0:15 - len(DIRECT)])
+    for d, here in zip(DIRECT, at_zero):
+        skipped = jnp.logical_and(z == 0, jnp.logical_and(c == d % CORES, jnp.logical_not(here)))
+
+        @pl.when(jnp.logical_not(skipped))
+        def _():
+            wait(ssend_sem.at[1], s_p.at[0])
+
+        @pl.when(jnp.logical_not(here))
+        def _():
+            wait(ssend_sem.at[2], s_d.at[0])
+
+    @pl.when(jnp.logical_not(direct))
+    def _():
+        wait(sp_sem, s_p.at[0:15])
+        s_all = s_p[0]
+        for k in range(1, SIDE * SIDE):
+            s_all = s_all + s_p[k]
+        total[:, 0:128] = s_all
+
+    @pl.when(direct)
+    def _():
+        wait(sd_sem, s_d.at[0:255])
+        column_sums = s_d[0:16]
+        for k in range(1, ZS * CORES):
+            column_sums = column_sums + s_d[16 * k:16 * k + 16]
+        s_all = column_sums[0]
+        for k in range(1, SIDE * SIDE):
+            s_all = s_all + column_sums[k]
+        total[:, 0:128] = s_all
 
 
 def tail_kernel(
@@ -389,6 +435,7 @@
             vector((4, 1, ROWS), f32),
             vector((16, 1, 256), f32),
             vector((16, 1, 128), f32),
+            vector((256, 1, 128), f32),
             dma((5,)),
             dma((8,)),
             dma((CHUNKS, 2)),
@@ -403,7 +450,8 @@
             dma,
             dma,
             dma,
-            dma((2,)),
+            dma((3,)),
+            dma,
             dma,
             dma,
             signal,

time: 34.1 us -> 33.7 us (0.988)
  Pallas kernels: 33.4 us -> 32.9 us
    pallas_call x1, Pallas kernels: 31.2 us -> 30.8 us  [on_device(): pl.pallas_call(comm_kernel, out_shape=(whole, whole, whole, jax.ShapeDtyp...]
where the time goes in v4:
time: 33.7 us; the launch traced here: 33.6 us
  Pallas kernels  32.9 us (98%)
  between operations  0.64 us (2%)
    pallas_call x1, Pallas kernels, on_device(): pl.pallas_call(comm_kernel, out_shape=(whole, whole, whole, jax.ShapeDtyp...  30.8 us
    pallas_call x1, Pallas kernels, on_device(): pl.pallas_call(tail_kernel, out_shape=(whole, whole, line, line), in_spec...  2.11 us

profile of v4, /device:TPU:1, one launch (start us, length us, event | category | flops | bytes accessed | tf_op | source)
XLA Modules:
  0.0 33.6 jit_solution(12097049664666580025)
XLA Ops:
  0.6 30.8 %worker_mean.1 = (f32[2,2,2,4,16,1024]{5,4,3,2,1,0:T(8,128)S(1)}, f32[2,2,2,4,16,1024]{5,4,3,2,1,0:T(8,128)S(1)}, f32[2,2,2,4,16,1024]{5,4,3,2,1,0:T(8,128)S(1)}...) custom-call(f32[2,2,2,4,16,1024]{5,4,3,2,1,0:T(8,128)} %bitcast.9, f32[1,512]{1,0:T(1,128)} %gd.1, ...), custom_call_target="tpu_custom_call" | custom-call | tf_op jit(solution)/shard_map/worker_mean/pallas_call | solution.py:415
  31.5 2.1 %apply_step.1 = (f32[2,2,2,4,16,1024]{5,4,3,2,1,0:T(8,128)}, f32[2,2,2,4,16,1024]{5,4,3,2,1,0:T(8,128)}, f32[1,512]{1,0:T(1,128)}, f32[1,512]{1,0:T(1,128)}) custom-call(f32[2,2,2,4,16,1024]{5,4,3,2,1,0:T(8,128)S(1)} %get-tuple-element.14.mom, f32[2,2,2,4,16,1024]{5,4,3,2,1,0:T(8,128)S(1)} %get-tuple-element.15.stp, ...), custom_call_target="tpu_custom_call" | custom-call | tf_op jit(solution)/shard_map/apply_step/pallas_call | solution.py:465

commit v5 on v4

--- a/solution.py
+++ b/solution.py
@@ -15,8 +15,9 @@
 OWN = SHAPE[1:]
 CUTS = [(True, 0, 8, 0, 512), (True, 0, 8, 512, 512), (True, 8, 8, 0, 512), (False, 8, 8, 512, 512)]
 CHUNKS = len(CUTS)
-EARLY = ZS // 2
-DIRECT = (1,)
+EARLY = 1
+SLACK = 1
+DIRECT = (1, 2, 8)
 MESH = pl.DeviceIdType.MESH
 
 
@@ -26,7 +27,7 @@
     acc, r0, r1a, r1b, r1, c2, r2, c3, avg, km,
     gd_v, gm_v, g_core, g_x, g_y, s_z, s_p, s_d,
     load_sem, send_sem, sem0, sem1a, sem1b, sem1, sem2, sem3, sem4, sem5,
-    gsend_sem, gc_sem, gx_sem, gy_sem, ssend_sem, sz_sem, sp_sem, sd_sem, ready_sem, go_sem,
+    gsend_sem, gc_sem, gx_sem, gy_sem, ssend_sem, sz_sem, sp_sem, sd_sem, ready_sem, go_sem, pair_sem,
 ):
     r = lax.axis_index("replica")
     z = lax.axis_index("fsdp")
@@ -56,8 +57,10 @@
             greet(sem, (at(x, y, q)[0], k))
 
     early = z < EARLY
-    for device in [sibling] + xpeer + ypeer:
-        greet(barrier, device)
+    for p in (2, 1, 3):
+        greet(barrier, at((x + p) % SIDE, y, 0))
+        greet(barrier, at(x, (y + p) % SIDE, 0))
+    pl.when(c == 0)(lambda: greet(barrier, sibling))
     for k in range(1, ZS):
         pl.when(jnp.logical_and(k > z, early))(lambda: greet_column(barrier, k))
 
@@ -80,7 +83,19 @@
     def wait(sem, like):
         pltpu.make_async_copy(like, like, sem).wait()
 
-    pl.semaphore_wait(barrier, 1 + 2 * (SIDE - 1) + CORES * jnp.minimum(z, EARLY))
+    lower = CORES * jnp.minimum(z, EARLY)
+
+    @pl.when(c == 1)
+    def _():
+        pl.semaphore_wait(barrier, 1 + lower)
+        greet(pair_sem, sibling)
+
+    @pl.when(c == 0)
+    def _():
+        pl.semaphore_wait(pair_sem, 1)
+
+    for k in range(EARLY):
+        pl.when(k < z)(lambda: greet_column(ready_sem, k))
 
     def cut(j):
         _, a, n, b, w = CUTS[j]
@@ -105,8 +120,15 @@
     send(gd_v, g_core, gsend_sem.at[0], gc_sem, sibling)
     for cp in loads[3:]:
         cp.start()
-    for k in range(EARLY):
-        pl.when(k < z)(lambda: greet_column(ready_sem, k))
+
+    @pl.when(c == 0)
+    def _():
+        pl.semaphore_wait(barrier, CORES * 2 * (SIDE - 1) + lower)
+        greet(pair_sem, sibling)
+
+    @pl.when(c == 1)
+    def _():
+        pl.semaphore_wait(pair_sem, 1)
 
     first = (x, y)
     second = (y, x)
@@ -203,10 +225,6 @@
     g_sq = g_step * g_step
     g_part = (g_sq[:, 0:128] + g_sq[:, 128:256]) + (g_sq[:, 256:384] + g_sq[:, 384:512])
 
-    @pl.when(early)
-    def _():
-        pl.semaphore_wait(ready_sem, CORES * (ZS - 1 - z))
-
     k_part = jnp.zeros((8, 128), jnp.float32)
     for j in range(CHUNKS):
         Rp, Cp = part(j)
@@ -227,11 +245,15 @@
                 for a in range(0, step.shape[0], 8):
                     for b in range(0, step.shape[1], 128):
                         k_part = k_part + square[a:a + 8, b:b + 128]
-        if j == 0:
-            @pl.when(z == 0)
-            def _():
-                for k in range(1, ZS):
-                    greet(go_sem, (r, k))
+
+    @pl.when(early)
+    def _():
+        pl.semaphore_wait(ready_sem, CORES * (ZS - 1 - z))
+
+    @pl.when(z == 0)
+    def _():
+        for k in range(1, ZS):
+            greet(go_sem, (r, k))
 
     @pl.when(z > 0)
     def _():
@@ -300,13 +322,14 @@
             return carry
         lax.fori_loop(0, 2 * SIDE, block, 0, unroll=2)
 
-    plane_round()
+    pl.when(z >= SLACK)(plane_round)
     for j in range(CHUNKS):
         R, C = cut(j)
         for o in range(2):
             wait(sem4.at[j, o], r1.at[o, :, :, R, C])
             blocks = avg.at[c, o, :, :, R, C]
             send(blocks, blocks, send_sem.at[7], sem5.at[j, o], sibling)
+    pl.when(z < SLACK)(plane_round)
     for j in range(CHUNKS):
         for o in range(2):
             finish(c, o, j)
@@ -456,6 +479,7 @@
             dma,
             signal,
             signal,
+            signal,
         ],
         compiler_params=pltpu.CompilerParams(
             collective_id=0, has_side_effects=True, vmem_limit_bytes=32 << 20

time: 33.7 us -> 33.6 us (level)
  Pallas kernels: 32.9 us -> 32.5 us
    pallas_call x1, Pallas kernels: 30.8 us -> 30.4 us  [on_device(): pl.pallas_call(comm_kernel, out_shape=(whole, whole, whole, jax.ShapeDtyp...]
where the time goes in v5:
time: 33.6 us; the launch traced here: 33.2 us
  Pallas kernels  32.5 us (97%)
  between operations  0.64 us (2%)
    pallas_call x1, Pallas kernels, on_device(): pl.pallas_call(comm_kernel, out_shape=(whole, whole, whole, jax.ShapeDtyp...  30.4 us
    pallas_call x1, Pallas kernels, on_device(): pl.pallas_call(tail_kernel, out_shape=(whole, whole, line, line), in_spec...  2.11 us

profile of v5, /device:TPU:1, one launch (start us, length us, event | category | flops | bytes accessed | tf_op | source)
XLA Modules:
  0.0 33.2 jit_solution(15835199213654812549)
XLA Ops:
  0.6 30.4 %worker_mean.1 = (f32[2,2,2,4,16,1024]{5,4,3,2,1,0:T(8,128)S(1)}, f32[2,2,2,4,16,1024]{5,4,3,2,1,0:T(8,128)S(1)}, f32[2,2,2,4,16,1024]{5,4,3,2,1,0:T(8,128)S(1)}...) custom-call(f32[2,2,2,4,16,1024]{5,4,3,2,1,0:T(8,128)} %bitcast.9, f32[1,512]{1,0:T(1,128)} %gd.1, ...), custom_call_target="tpu_custom_call" | custom-call | tf_op jit(solution)/shard_map/worker_mean/pallas_call | solution.py:438
  31.1 2.1 %apply_step.1 = (f32[2,2,2,4,16,1024]{5,4,3,2,1,0:T(8,128)}, f32[2,2,2,4,16,1024]{5,4,3,2,1,0:T(8,128)}, f32[1,512]{1,0:T(1,128)}, f32[1,512]{1,0:T(1,128)}) custom-call(f32[2,2,2,4,16,1024]{5,4,3,2,1,0:T(8,128)S(1)} %get-tuple-element.14.mom, f32[2,2,2,4,16,1024]{5,4,3,2,1,0:T(8,128)S(1)} %get-tuple-element.15.stp, ...), custom_call_target="tpu_custom_call" | custom-call | tf_op jit(solution)/shard_map/apply_step/pallas_call | solution.py:489

commit v6 on v4

--- a/solution.py
+++ b/solution.py
@@ -15,8 +15,9 @@
 OWN = SHAPE[1:]
 CUTS = [(True, 0, 8, 0, 512), (True, 0, 8, 512, 512), (True, 8, 8, 0, 512), (False, 8, 8, 512, 512)]
 CHUNKS = len(CUTS)
-EARLY = ZS // 2
-DIRECT = (1,)
+EARLY = 1
+SLACK = 1
+DIRECT = (1, 2, 8)
 MESH = pl.DeviceIdType.MESH
 
 
@@ -300,13 +301,14 @@
             return carry
         lax.fori_loop(0, 2 * SIDE, block, 0, unroll=2)
 
-    plane_round()
+    pl.when(z >= SLACK)(plane_round)
     for j in range(CHUNKS):
         R, C = cut(j)
         for o in range(2):
             wait(sem4.at[j, o], r1.at[o, :, :, R, C])
             blocks = avg.at[c, o, :, :, R, C]
             send(blocks, blocks, send_sem.at[7], sem5.at[j, o], sibling)
+    pl.when(z < SLACK)(plane_round)
     for j in range(CHUNKS):
         for o in range(2):
             finish(c, o, j)

time: 33.7 us -> 33.4 us (level); the launches traced: 33.6 us -> 32.8 us
  Pallas kernels: 32.9 us -> 32.2 us
    pallas_call x1, Pallas kernels: 30.8 us -> 30.1 us  [on_device(): pl.pallas_call(comm_kernel, out_shape=(whole, whole, whole, jax.ShapeDtyp...]
where the time goes in v6:
time: 33.4 us; the launch traced here: 32.8 us
  Pallas kernels  32.2 us (96%)
  between operations  0.64 us (2%)
    pallas_call x1, Pallas kernels, on_device(): pl.pallas_call(comm_kernel, out_shape=(whole, whole, whole, jax.ShapeDtyp...  30.1 us
    pallas_call x1, Pallas kernels, on_device(): pl.pallas_call(tail_kernel, out_shape=(whole, whole, line, line), in_spec...  2.11 us

profile of v6, /device:TPU:1, one launch (start us, length us, event | category | flops | bytes accessed | tf_op | source)
XLA Modules:
  0.0 32.8 jit_solution(295878992515463459)
XLA Ops:
  0.6 30.1 %worker_mean.1 = (f32[2,2,2,4,16,1024]{5,4,3,2,1,0:T(8,128)S(1)}, f32[2,2,2,4,16,1024]{5,4,3,2,1,0:T(8,128)S(1)}, f32[2,2,2,4,16,1024]{5,4,3,2,1,0:T(8,128)S(1)}...) custom-call(f32[2,2,2,4,16,1024]{5,4,3,2,1,0:T(8,128)} %bitcast.9, f32[1,512]{1,0:T(1,128)} %gd.1, ...), custom_call_target="tpu_custom_call" | custom-call | tf_op jit(solution)/shard_map/worker_mean/pallas_call | solution.py:417
  30.7 2.1 %apply_step.1 = (f32[2,2,2,4,16,1024]{5,4,3,2,1,0:T(8,128)}, f32[2,2,2,4,16,1024]{5,4,3,2,1,0:T(8,128)}, f32[1,512]{1,0:T(1,128)}, f32[1,512]{1,0:T(1,128)}) custom-call(f32[2,2,2,4,16,1024]{5,4,3,2,1,0:T(8,128)S(1)} %get-tuple-element.14.mom, f32[2,2,2,4,16,1024]{5,4,3,2,1,0:T(8,128)S(1)} %get-tuple-element.15.stp, ...), custom_call_target="tpu_custom_call" | custom-call | tf_op jit(solution)/shard_map/apply_step/pallas_call | solution.py:467
